TPU v7x, 32 devices: a whole 2x2x4 slice. The times are simulated.
32 devices in a mesh: mol: 8 (over y, x, core), row: 4 (over z).
Axes of the slice: x: 2, y: 2, z: 4, core: 2. Of those that a mesh axis runs over, the one named last changes fastest.
Arguments:
- node_states: bfloat16 [3712, 128], P('mol'), may hold values from -6 to 6
- edge_feats: bfloat16 [65536, 16], P('mol'), may hold values from -6 to 6
- edge_src: int32 [65536], P('mol'), may hold values from 0 to 3711, as said below
- edge_dst: int32 [65536], P('mol'), may hold values from 0 to 3711, as said below
- atom_counts: int32 [128], P('mol'), may hold values from 9 to 29, as said below
- edge_counts: int32 [128], P('mol'), may hold values from 1 to 512, as said below
- mol_group: int32 [128], P('mol'), may hold values from 0 to 1
- col_mask: int32 [2, 16], replicated, may hold values 0 or 1
- cotangent: bfloat16 [3712, 128], P('mol'), may hold values from -6 to 6
- edge_in_state: float32 [3, 16, 128], replicated
- edge_in_bias_state: float32 [3, 128], replicated
- edge_out_state: float32 [3, 128, 16384], P(None, 'mol', 'row')
- edge_out_bias_state: float32 [3, 16384], P(None, 'row')
- gate_in_state: float32 [3, 128, 384], replicated
- gate_hidden_state: float32 [3, 128, 384], replicated
- gate_bias_state: float32 [3, 2, 384], replicated
Outputs:
- states: float32 [3712, 128], P('mol')
- state_grad: float32 [3712, 128], P('mol')
- edge_in_grad: float32 [16, 128], replicated
- edge_in_new: float32 [3, 16, 128], replicated
- edge_in_bias_grad: float32 [128], replicated
- edge_in_bias_new: float32 [3, 128], replicated
- edge_out_grad: float32 [128, 16384], P('mol', 'row')
- edge_out_new: float32 [3, 128, 16384], P(None, 'mol', 'row')
- edge_out_bias_grad: float32 [16384], P('row')
- edge_out_bias_new: float32 [3, 16384], P(None, 'row')
- gate_in_grad: float32 [128, 384], replicated
- gate_in_new: float32 [3, 128, 384], replicated
- gate_hidden_grad: float32 [128, 384], replicated
- gate_hidden_new: float32 [3, 128, 384], replicated
- gate_bias_grad: float32 [2, 384], replicated
- gate_bias_new: float32 [3, 2, 384], replicated
Inputs may be any that keep to these rules, and one draw needn't show every extreme that they name: `atom_counts`: each index of mol holds 16 consecutive molecules, and the last of them has 29 atoms. `edge_counts`: molecule k has at most atom_counts[k] * (atom_counts[k] - 1) edges; on each index of mol the last of its molecules has 512 edges. `edge_src`: edge slot k * 512 + j names atom slot k * 29 + a with a < atom_counts[k] when j < edge_counts[k], and k * 29 otherwise. `edge_dst`: as edge_src; a live edge's destination differs from its source.
All inputs are finite; a program needn't handle non-finite values.
Results may differ from a plain program's by a relative error of at most 0.015.
The roundings to bfloat16 on the way count: a program that leaves them out, or rounds other values in their place, can miss the bound.
Values may be sent and summed in bfloat16 or wider, within the bound.
A program may use at most 64 MiB of HBM per device.

v0:
```python
import functools
from typing import Any, NamedTuple

import jax
import jax.numpy as jnp
import numpy as np
from jax import lax
from jax.experimental import pallas as pl
from jax.experimental.pallas import tpu as pltpu
from jax.sharding import PartitionSpec as P

LAYERS = 2
HALF = 8
LANES = 128
PARTS = 2
MOL, ROW = "mol", "row"
MESH = pl.DeviceIdType.MESH
VMEM_BYTES = 58 * 1024 * 1024

momentum_coef = 0.9
average_decay = 0.9
f32 = jnp.float32
bf16 = jnp.bfloat16


def dot(left, right):
    return lax.dot_general(left, right, (((1,), (0,)), ((), ())), preferred_element_type=f32)


def dot_nt(left, right):
    return lax.dot_general(left, right, (((1,), (1,)), ((), ())), preferred_element_type=f32)


def dot_tn(left, right):
    return lax.dot_general(left, right, (((0,), (0,)), ((), ())), preferred_element_type=f32)


def low(value):
    return value.astype(bf16)


def iota(shape, axis):
    return lax.broadcasted_iota(jnp.int32, shape, axis)


def hot(mask):
    return low(jnp.where(mask, 1.0, 0.0))


class Sizes:
    def __init__(self, mesh, node_states, edge_feats, atom_counts, edge_in_state, edge_out_bias_state):
        self.n_mol, self.n_row = mesh.shape["mol"], mesh.shape["row"]
        self.mols = atom_counts.shape[0]
        self.nodes, self.width = node_states.shape
        self.cap = self.nodes // self.mols
        self.edges = edge_feats.shape[0] // self.mols
        self.feats = edge_feats.shape[1]
        self.units = edge_in_state.shape[2]
        self.rows = edge_out_bias_state.shape[1] // self.width
        self.per = self.units // self.n_mol
        self.halves = self.mols // HALF
        self.vpad = 32
        self.wpad = self.cap + self.cap % 2
        self.lanes = self.mols * self.vpad
        self.half_lanes = HALF * self.vpad
        self.half_rows = HALF * self.wpad
        self.span = self.wpad * self.units
        self.fused = self.per % 16 == 0
        self.gate_rows = 6 * self.width
        self.small_rows = self.gate_rows + 16 + self.rows
        self.chunk = -(-self.small_rows // (16 * self.n_mol)) * 16


class Operands(NamedTuple):
    nodes: Any
    feats_t: Any
    src: Any
    dst: Any
    atoms: Any
    edges: Any
    group: Any
    col_mask: Any
    cot: Any
    w1: Any
    b1: Any
    w2: Any
    b2: Any
    wi: Any
    wh: Any
    bg: Any
    perm_in_c: Any
    perm_c: Any


class Results(NamedTuple):
    states: Any
    state_grad: Any
    out_rows: Any
    small_out: Any
    w1_out: Any


class Scratch(NamedTuple):
    nodes_v: Any
    feats_v: Any
    src_v: Any
    dst_v: Any
    cot_v: Any
    w2_v: Any
    wi_v: Any
    wh_v: Any
    perm_in: Any
    perm: Any
    w2s: Any
    w2t: Any
    stage: Any
    hid: Any
    idx: Any
    s2: Any
    counts: Any
    cnt: Any
    t2: Any
    d2: Any
    e2: Any
    e_acc: Any
    dw_acc: Any
    ob_acc: Any
    live: Any
    h: Any
    hb: Any
    hbw: Any
    hbw_t: Any
    gates: Any
    mt: Any
    dmt: Any
    dmn: Any
    dm: Any
    dgi: Any
    dgh: Any
    wib: Any
    whb: Any
    wit: Any
    wht: Any
    bcol: Any
    gt: Any
    spart: Any
    rs_in: Any
    sred: Any
    dwp: Any
    dw_in: Any
    dw_mid: Any
    dw_in2: Any
    sm_part: Any
    sm_in: Any
    sm_red: Any
    w1_part: Any
    w1_in: Any
    w1_mid: Any
    w1_in2: Any
    col_mask_v: Any
    w1_v: Any
    b1_v: Any
    bg_v: Any
    b2_v: Any
    group_s: Any
    edges_s: Any
    atoms_s: Any
    states_v: Any
    state_grad_v: Any
    out_rows_v: Any
    lsem: Any
    osem: Any
    w2_send: Any
    w2_recv: Any
    w2_fsend: Any
    m_send: Any
    m_recv: Any
    rs_send: Any
    rs_recv: Any
    ag_send: Any
    ag_recv: Any
    dw_send: Any
    dw_recv: Any
    dw2_send: Any
    dw2_recv: Any
    sm_send: Any
    sm_recv: Any
    sa_send: Any
    sa_recv: Any
    wr_send: Any
    wr_recv: Any
    wm_send: Any
    wm_recv: Any


def step_kernel(z, *refs):
    n_in, n_out = len(Operands._fields), len(Results._fields)
    a = Operands(*refs[:n_in])
    o = Results(*refs[n_in : n_in + n_out])
    r = Scratch(*refs[n_in + n_out :])
    atoms, edges, group = r.atoms_s, r.edges_s, r.group_s
    me, row = lax.axis_index(MOL), lax.axis_index(ROW)
    n_mol, n_row, rows, units, per = z.n_mol, z.n_row, z.rows, z.units, z.per
    width, halves = z.width, range(z.halves)
    row_at = pl.multiple_of(row * rows, rows)

    def others(index, count):
        return [lax.rem(index + step, count) for step in range(1, count)]

    mol_peers, row_peers = others(me, n_mol), others(row, n_row)

    def remote(source, target, send, recv, axis, device):
        return pltpu.make_async_remote_copy(
            src_ref=source,
            dst_ref=target,
            send_sem=send,
            recv_sem=recv,
            device_id={axis: device},
            device_id_type=MESH,
        )

    sent, stored = [], []

    def push(*args):
        remote(*args).start()
        sent.append(args)

    def store(source, target):
        pltpu.make_async_copy(source, target, r.osem.at[len(stored)]).start()
        stored.append((source, target))

    def arrived(there, send, recv, axis, device):
        remote(there, there, send, recv, axis, device).wait_recv()

    started = []

    def fetch(source, target):
        copy = pltpu.make_async_copy(source, target, r.lsem.at[len(started)])
        copy.start()
        started.append(copy)
        return copy

    barrier = pltpu.get_barrier_semaphore()
    for peer in mol_peers:
        pl.semaphore_signal(barrier, inc=1, device_id={MOL: peer}, device_id_type=MESH)
    for peer in row_peers:
        pl.semaphore_signal(barrier, inc=1, device_id={ROW: peer}, device_id_type=MESH)
    in_w2 = fetch(a.w2.at[0], r.w2_v) if z.fused else fetch(a.w2, r.w2s)
    in_small = (
        fetch(a.col_mask, r.col_mask_v),
        fetch(a.w1.at[0], r.w1_v),
        fetch(a.b1, r.b1_v),
        fetch(a.group, r.group_s),
        fetch(a.edges, r.edges_s),
        fetch(a.atoms, r.atoms_s),
    )
    in_src, in_dst = fetch(a.src, r.src_v), fetch(a.dst, r.dst_v)
    in_feats, in_nodes = fetch(a.feats_t, r.feats_v), fetch(a.nodes, r.nodes_v)
    in_perms = fetch(a.perm_in_c, r.perm_in), fetch(a.perm_c, r.perm)
    in_wi, in_wh = fetch(a.wi.at[0], r.wi_v), fetch(a.wh.at[0], r.wh_v)
    in_cot = fetch(a.cot, r.cot_v)
    in_bg, in_b2 = fetch(a.bg.at[0], r.bg_v), fetch(a.b2, r.b2_v)

    w2s, stage = r.w2s, r.stage
    partner = me + 1 - 2 * lax.rem(me, 2)
    same = [lax.rem(me + 2 * step, n_mol) for step in range(1, n_mol // 2)]
    same_of_partner = [lax.rem(partner + 2 * step, n_mol) for step in range(1, n_mol // 2)]

    some = rows // PARTS

    def block_of(ref, owner):
        return ref.at[:, pl.ds(pl.multiple_of(owner * per, 16), per), :]

    def part_of(owner, part):
        return w2s.at[pl.ds(part * some, some), pl.ds(pl.multiple_of(owner * per, 16), per), :]

    def forwards(part):
        copies = []
        for at, peer in enumerate(same):
            there, recv = part_of(peer, part), r.w2_recv.at[part, peer]
            copies.append(remote(there, there, r.w2_fsend.at[part, at], recv, MOL, partner))
        return copies

    def forward_part(part):
        for at, (peer, copy) in enumerate(zip(same, forwards(part))):
            there = part_of(peer, part)
            arrived(there, r.w2_send.at[part, at], r.w2_recv.at[part, peer], MOL, peer)
            copy.start()

    def whole_part(part):
        for peer in [partner] + same_of_partner:
            there = part_of(peer, part)
            arrived(there, r.w2_send.at[part, 0], r.w2_recv.at[part, peer], MOL, partner)

    for copy in in_small:
        copy.wait()
    lane_mol = iota((1, z.lanes), 1) // z.vpad
    lane_v = lax.rem(iota((1, z.lanes), 1), z.vpad)
    half_mol = iota((HALF, z.half_lanes), 1) // z.vpad == iota((HALF, z.half_lanes), 0)
    fold = hot(iota((rows, rows * HALF), 1) // HALF == iota((rows, rows * HALF), 0))
    tile_v = hot(lax.rem(iota((z.vpad, z.half_lanes), 1), z.vpad) == iota((z.vpad, z.half_lanes), 0))
    live_to = jnp.zeros((1, z.lanes), jnp.int32)
    for m in range(z.mols):
        live_to = jnp.where(lane_mol == m, atoms[m], live_to)
    live_all = jnp.where(lane_v < live_to, 1.0, 0.0)
    for half in halves:
        lanes = slice(half * z.half_lanes, (half + 1) * z.half_lanes)
        r.live[half] = jnp.broadcast_to(live_all[:, lanes], (8, z.half_lanes))
    r.e_acc[...] = jnp.zeros(r.e_acc.shape, f32)
    r.dw_acc[...] = jnp.zeros(r.dw_acc.shape, f32)
    r.ob_acc[...] = jnp.zeros(r.ob_acc.shape, f32)

    mask_cols = jnp.concatenate(
        [r.col_mask_v[...].astype(f32), jnp.zeros((8 - a.col_mask.shape[0], z.feats), f32)], axis=0
    )
    mask_cols = jnp.concatenate([mask_cols, jnp.zeros((8, LANES - z.feats), f32)], axis=1).T
    masks = [low(jnp.broadcast_to(mask_cols[: z.feats, g : g + 1], (z.feats, z.edges))) for g in (0, 1)]
    w1_low = low(r.w1_v[...])
    b1_row = r.b1_v[0:1, :]

    if z.fused:
        in_w2.wait()
        for i in range(rows):
            stage[i] = low(r.w2_v[:, i * LANES : (i + 1) * LANES])
        w2s[:, pl.ds(pl.multiple_of(me * per, 16), per), :] = stage[...]
    pl.semaphore_wait(barrier, n_mol - 1 + n_row - 1)
    if z.fused:
        for part in range(PARTS):
            for at, peer in enumerate(same + [partner]):
                push(
                    stage.at[pl.ds(part * some, some)],
                    part_of(me, part),
                    r.w2_send.at[part, at],
                    r.w2_recv.at[part, me],
                    MOL,
                    peer,
                )

    s2, hid, idx, counts = r.s2, r.hid, r.idx, r.counts
    for copy in (in_src, in_dst, in_feats):
        copy.wait()
    lines = z.edges // LANES
    edge_at = iota((1, z.edges), 1)
    v_id = low(iota((z.vpad, z.edges), 0).astype(f32))
    one, zero = jnp.ones((), bf16), jnp.zeros((), bf16)

    def pair_hots(ends, count):
        from_all = low(jnp.broadcast_to(ends[0:1], (z.vpad, z.edges)))
        to_all = low(jnp.broadcast_to(ends[1:2], (z.vpad, z.edges)))
        to_hot = jnp.where(to_all == v_id, one, zero)
        from_hot = jnp.where(from_all == v_id, one, zero)
        pair_hot = [
            jnp.where(from_all == jnp.full((), w, bf16), to_hot, zero) for w in range(count)
        ]
        return from_hot, to_hot, jnp.concatenate(pair_hot, axis=0)

    def one_molecule(half, m8):
        m = half * HALF + m8
        at = pl.multiple_of(m * z.edges, z.edges)
        base = (me * z.mols + m) * z.cap
        kept = jnp.where(group[m] == 1, masks[1], masks[0])
        feats_m = r.feats_v[:, pl.ds(at, z.edges)] * kept
        r.feats_v[:, pl.ds(at, z.edges)] = feats_m
        hidden = low(jnp.maximum(dot_tn(feats_m, w1_low) + b1_row, 0.0))
        hid[m] = hidden.T

        def line(ref):
            return jnp.concatenate(
                [ref[pl.ds(m * lines + t, 1), :] for t in range(lines)], axis=1
            )

        from_at = line(r.src_v) - base
        to_at = jnp.where(edge_at < edges[m], line(r.dst_v) - base, 2 * z.vpad)
        ends = jnp.concatenate([from_at, to_at, jnp.zeros((6, z.edges), jnp.int32)], axis=0)
        ends = ends.astype(f32)
        idx[m] = ends
        from_hot, to_hot, pair_hot = pair_hots(ends, z.cap)
        sums = low(dot(pair_hot, hidden))
        for w in range(z.cap):
            s2[half, m8 * z.vpad : (m8 + 1) * z.vpad, w * units : (w + 1) * units] = sums[
                w * z.vpad : (w + 1) * z.vpad
            ]
        found = dot(low(dot_nt(from_hot, to_hot)), tile_v)
        found = jnp.where(iota(found.shape, 1) // z.vpad == m8, found, 0.0)
        counts[half, :, m8 : m8 + 1, :] = found[: z.wpad].reshape(z.wpad, 1, z.half_lanes)

    def half_sums(half, carry):
        s2[half, :, z.cap * units :] = jnp.zeros((z.half_lanes, (z.wpad - z.cap) * units), bf16)
        for m8 in range(HALF):
            if z.fused and m8 == HALF - 2:
                pl.when(half == z.halves - 1)(functools.partial(forward_part, 0))
            one_molecule(half, m8)
        r.cnt[half] = low(counts[half].reshape(z.half_rows, z.half_lanes))
        return carry

    lax.fori_loop(0, z.halves, half_sums, 0)
    if z.fused:
        for part in range(1, PARTS):
            forward_part(part)

    h, hb, hbw, hbw_t = r.h, r.hb, r.hbw, r.hbw_t
    for copy in (in_nodes, *in_perms):
        copy.wait()

    def set_rows(layer, half):
        hb[layer, half] = low(h[layer, half])
        hbw[layer, half] = low(dot_nt(r.perm[...], hb[layer, half]))
        hbw_t[layer, half] = low(dot_nt(hb[layer, half], r.perm[...]))

    def rows_in(value, target):
        moved = dot_tn(value, r.perm_in[...])
        for half in halves:
            target[half] = moved[:, half * z.half_lanes : (half + 1) * z.half_lanes]

    rows_in(r.nodes_v[...], h.at[0])
    for half in halves:
        set_rows(0, half)
    wib, whb, wit, wht, bcol = r.wib, r.whb, r.wit, r.wht, r.bcol
    in_b2.wait()
    b2_low = low(
        jnp.concatenate([r.b2_v[0:1, i * LANES : (i + 1) * LANES] for i in range(rows)], axis=0)
    )

    if not z.fused:
        in_w2.wait()

    t2, mt, gates, w2t = r.t2, r.mt, r.gates, r.w2t

    def two(at):
        return slice(at * 2 * units, (at + 1) * 2 * units)

    def wide(block):
        return jnp.concatenate([block] * (z.half_lanes // LANES), axis=1)

    def spread(layer, half, part):
        state = hbw[layer, half]

        def pair(at):
            ip = part * (some // 2) + at
            both = dot_nt(state, w2s[2 * ip : 2 * ip + 2].reshape(2 * units, width))
            at = ip * 2 * HALF
            for w in range(z.wpad):
                s = slice(w * HALF, (w + 1) * HALF)
                t2[layer, half, pl.ds(at, 2 * HALF), w * units : (w + 1) * units] = low(
                    jnp.concatenate([both[s, :units], both[s, units:]], axis=0)
                )

        for at in range(some // 2):
            pair(at)

    def messages(layer, half):
        state = hbw[layer, half]
        bias = dot(low(dot_nt(b2_low, state)), r.cnt[half])
        full = dot_nt(t2[layer, half], s2[half]).reshape(rows, HALF, z.half_lanes)
        full = jnp.where(half_mol[None], full + bias[:, None, :], 0.0)
        full = low(full.reshape(rows * HALF, z.half_lanes))
        mt[layer, half, pl.ds(row_at, rows), :] = low(dot(fold, full))
        share(mt, r.m_send, r.m_recv, layer, half)

    def row_pushes(ref, send, recv, layer, half):
        mine = ref.at[layer, half, pl.ds(row_at, rows), :]
        return [
            remote(mine, mine, send.at[layer, half, at], recv.at[layer, half, row], ROW, peer)
            for at, peer in enumerate(row_peers)
        ]

    def share(*args):
        for copy in row_pushes(*args):
            copy.start()

    def collect(ref, send, recv, layer, half):
        for peer in row_peers:
            there = ref.at[layer, half, pl.ds(pl.multiple_of(peer * rows, rows), rows), :]
            arrived(there, send.at[layer, half, 0], recv.at[layer, half, peer], ROW, peer)

    def state_side(layer, half):
        gates[layer, half, 0] = dot(wht[...], hb[layer, half]) + wide(bcol[1])

    def gru(layer, half):
        collect(mt, r.m_send, r.m_recv, layer, half)
        from_msg = dot(wit[...], mt[layer, half]) + wide(bcol[0])
        from_state = gates[layer, half, 0]
        reset = jax.nn.sigmoid(from_msg[:width] + from_state[:width])
        update = jax.nn.sigmoid(from_msg[width : 2 * width] + from_state[width : 2 * width])
        new = jnp.tanh(from_msg[2 * width :] + reset * from_state[2 * width :])
        gates[layer, half, 1, :width] = reset
        gates[layer, half, 1, width : 2 * width] = update
        gates[layer, half, 1, 2 * width :] = new
        h[layer + 1, half] = r.live[half, 0:1] * ((1.0 - update) * new + update * h[layer, half])

    gt, dgi, dgh, dm, dmt, dmn = r.gt, r.dgi, r.dgh, r.dm, r.dmt, r.dmn
    d2, spart, sred = r.d2, r.spart, r.sred

    def gru_back(layer, half):
        up = gt[half] * r.live[half, 0:1]
        reset = gates[layer, half, 1, :width]
        update = gates[layer, half, 1, width : 2 * width]
        new = gates[layer, half, 1, 2 * width :]
        d_new = up * (1.0 - update) * (1.0 - new * new)
        d_update = up * (h[layer, half] - new) * update * (1.0 - update)
        d_reset = d_new * gates[layer, half, 0, 2 * width :] * reset * (1.0 - reset)
        msg_side = low(jnp.concatenate([d_reset, d_update, d_new], axis=0))
        dgi[layer, half] = msg_side
        dgh[layer, half, : 2 * width] = msg_side[: 2 * width]
        dgh[layer, half, 2 * width :] = low(d_new * reset)
        part = low(dot(wib[pl.ds(row_at, rows), :], msg_side))
        dm[layer, half] = part
        spread = jnp.where(half_mol[None], part.astype(f32)[:, None, :], 0.0)
        spread = spread.reshape(rows * HALF, z.half_lanes)
        dmt[layer, half] = low(spread)
        dmn[layer, half] = low(spread.T)
        gt[half] = up * update + dot(whb[...], dgh[layer, half])

    def gathered(layer, half):
        def pair(wp):
            lanes = two(wp)
            both = dot(dmt[layer, half], s2[half, :, lanes])
            at = wp * 2 * HALF
            for i in range(rows):
                part = both[i * HALF : (i + 1) * HALF]
                d2[pl.ds(at, 2 * HALF), i * units : (i + 1) * units] = low(
                    jnp.concatenate([part[:, :units], part[:, units:]], axis=0)
                )

        for wp in range(z.wpad // 2):
            pair(wp)

    def bias_rows(layer, half):
        return low(dot_nt(dm[layer, half], r.cnt[half]))

    def state_part(layer, half):
        biases = bias_rows(layer, half)
        r.ob_acc[...] += dot(biases, hbw[layer, half])
        back = dot_nt(w2t[...], d2[...]) + dot_tn(b2_low, biases)
        spart[layer, half] = low(dot(low(back), r.perm[...]))
        for copy in part_pushes(layer, half):
            copy.start()

    def part_pushes(layer, half):
        return [
            remote(
                spart.at[layer, half, pl.ds(pl.multiple_of(peer * rows, rows), rows), :],
                r.rs_in.at[layer, half, row],
                r.rs_send.at[layer, half, at],
                r.rs_recv.at[layer, half, row],
                ROW,
                peer,
            )
            for at, peer in enumerate(row_peers)
        ]

    def state_sum(layer, half):
        total = spart[layer, half, pl.ds(row_at, rows), :].astype(f32)
        for peer in row_peers:
            there = r.rs_in.at[layer, half, peer]
            arrived(there, r.rs_send.at[layer, half, 0], r.rs_recv.at[layer, half, peer], ROW, peer)
            total = total + r.rs_in[layer, half, peer].astype(f32)
        sred[layer, half, pl.ds(row_at, rows), :] = low(total)
        share(sred, r.ag_send, r.ag_recv, layer, half)

    def settle():
        def one_step(t, carry):
            layer, half = lax.div(t, z.halves), lax.rem(t, z.halves)
            for copy in row_pushes(mt, r.m_send, r.m_recv, layer, half):
                copy.wait_send()
            for copy in part_pushes(layer, half):
                copy.wait_send()
            for copy in row_pushes(sred, r.ag_send, r.ag_recv, layer, half):
                copy.wait_send()
            return carry

        lax.fori_loop(0, LAYERS * z.halves, one_step, 0)
        for args in sent:
            remote(*args).wait_send()
        for copy in small_copies():
            copy.wait_send()
        if z.fused:
            for copy in owner_copies():
                copy.wait_send()
            for part in range(PARTS):
                for copy in forwards(part):
                    copy.wait_send()

    def rows_out(value):
        total = None
        for half in halves:
            rest = value(half)
            lanes = slice(half * z.half_lanes, (half + 1) * z.half_lanes)
            for _ in range(3):
                part = low(rest)
                rest = rest - part.astype(f32)
                moved = dot_nt(r.perm_in[:, lanes], part)
                total = moved if total is None else total + moved
        return total

    dwp, dw_acc, e2, e_acc = r.dwp, r.dw_acc, r.e2, r.e_acc

    def weight_grad(layer, half):
        for ip in range(rows // 2):
            at = two(ip)
            dw_acc[:, at] += dot(hbw_t[layer, half], d2[:, at])

    def pair_grad(layer, half):
        for wp in range(z.wpad // 2):
            at = two(wp)
            total = e_acc[half, :, at] + dot(dmn[layer, half], t2[layer, half, :, at])
            e_acc[half, :, at] = total
            e2[half, :, at] = low(total)

    def gate_weights():
        in_wi.wait()
        in_wh.wait()
        wib[...] = low(r.wi_v[...])
        whb[...] = low(r.wh_v[...])
        wit[...] = low(r.wi_v[...].T)
        wht[...] = low(r.wh_v[...].T)
        in_cot.wait()
        in_bg.wait()
        bias_t = jnp.concatenate([r.bg_v[...], jnp.zeros((6, 3 * width), f32)], axis=0).T
        for side in range(2):
            bcol[side] = jnp.broadcast_to(bias_t[:, side : side + 1], (3 * width, LANES))
        rows_in(r.cot_v[...], r.gt)
        for i in range(rows):
            w2t[:, i * units : (i + 1) * units] = w2s[i].T
        for half in halves:
            state_side(0, half)

    def forward_step(t, carry):
        layer, half = lax.div(t, z.halves), lax.rem(t, z.halves)

        @pl.when(layer > 0)
        def _():
            gru(layer - 1, half)
            set_rows(layer, half)

        for part in range(PARTS):
            if z.fused and part > 0:
                pl.when(t == 0)(functools.partial(whole_part, part))
            spread(layer, half, part)
        messages(layer, half)
        pl.when(t == z.halves - 1)(gate_weights)
        pl.when(layer > 0)(functools.partial(state_side, layer, half))
        return carry

    if z.fused:
        whole_part(0)
    lax.fori_loop(0, LAYERS * z.halves, forward_step, 0)

    last = LAYERS - 1

    def back_half(layer, half):
        @pl.when(layer == last)
        def _():
            gru(last, half)

        @pl.when(layer < last)
        def _():
            collect(sred, r.ag_send, r.ag_recv, layer + 1, half)
            gt[half] += sred[layer + 1, half].astype(f32)

        gru_back(layer, half)
        gathered(layer, half)
        state_part(layer, half)
        weight_grad(layer, half)

    def pair_half(layer, half):
        pair_grad(layer, half)

        @pl.when(layer == last)
        def _():
            state_sum(last, half)

    def backward_layer(t, carry):
        layer = last - t
        lax.fori_loop(0, z.halves, lambda half, c: back_half(layer, half) or c, 0)
        lax.fori_loop(0, z.halves, lambda half, c: pair_half(layer, half) or c, 0)

        @pl.when(layer == last)
        def _():
            r.states_v[...] = rows_out(lambda half: h[LAYERS, half])
            store(r.states_v, o.states)

        return carry

    lax.fori_loop(0, LAYERS, backward_layer, 0)

    for i in range(rows):
        dwp[i] = low(dw_acc[:, i * units : (i + 1) * units].T)
    theirs = [lax.rem(partner + 2 * step, n_mol) for step in range(n_mol // 2)]
    ours = [lax.rem(me + 2 * step, n_mol) for step in range(n_mol // 2)]
    if z.fused:
        for at, owner in enumerate(theirs):
            push(block_of(dwp, owner), r.dw_in.at[at], r.dw_send.at[at], r.dw_recv.at[at], MOL, partner)

    sm_part, sm_in, sm_red = r.sm_part, r.sm_in, r.sm_red
    every = [(layer, half) for layer in range(LAYERS) for half in halves]

    def summed(pieces):
        return functools.reduce(jnp.add, pieces)

    def beside(ref):
        return jnp.concatenate([ref[e] for e in every], axis=1)

    for at, (side, grads) in enumerate(((mt, dgi), (hb, dgh))):
        total = dot_nt(beside(side), beside(grads))
        for third in range(3):
            first = (3 * at + third) * width
            sm_part[first : first + width, :] = low(total[:, third * width : (third + 1) * width])
    ones = jnp.ones((8, len(every) * z.half_lanes), bf16)
    bias_lines = []
    for grads in (dgi, dgh):
        total = dot_nt(ones, beside(grads))
        bias_lines += [total[0:1, third * width : (third + 1) * width] for third in range(3)]
    bias_lines.append(jnp.zeros((10, width), f32))
    sm_part[z.gate_rows : z.gate_rows + 16, :] = low(jnp.concatenate(bias_lines, axis=0))
    sm_part[z.gate_rows + 16 : z.small_rows, :] = low(r.ob_acc[...])
    if z.chunk * n_mol > z.small_rows:
        sm_part[z.small_rows :, :] = jnp.zeros((z.chunk * n_mol - z.small_rows, width), bf16)

    def chunk_of(ref, owner):
        return ref.at[pl.ds(pl.multiple_of(owner * z.chunk, 16), z.chunk), :]

    for at, peer in enumerate(mol_peers):
        push(chunk_of(sm_part, peer), sm_in.at[me], r.sm_send.at[at], r.sm_recv.at[me], MOL, peer)

    def owner_copies():
        return [
            remote(r.dw_mid.at[at], r.dw_in2.at[at], r.dw2_send.at[at], r.dw2_recv.at[at], MOL, owner)
            for at, owner in enumerate(ours)
            if at > 0
        ]

    def small_copies():
        mine = chunk_of(sm_red, me)
        return [
            remote(mine, mine, r.sa_send.at[at], r.sa_recv.at[me], MOL, peer)
            for at, peer in enumerate(mol_peers)
        ]

    def between():
        if z.fused:
            for at, owner in enumerate(ours):
                arrived(r.dw_in.at[at], r.dw_send.at[at], r.dw_recv.at[at], MOL, partner)
                own = dwp[:, pl.ds(pl.multiple_of(owner * per, 16), per), :].astype(f32)
                r.dw_mid[at] = low(own + r.dw_in[at].astype(f32))
                if at > 0:
                    owner_copies()[at - 1].start()
        total = sm_part[pl.ds(pl.multiple_of(me * z.chunk, 16), z.chunk), :].astype(f32)
        for peer in mol_peers:
            arrived(sm_in.at[peer], r.sm_send.at[0], r.sm_recv.at[peer], MOL, peer)
            total = total + sm_in[peer].astype(f32)
        sm_red[pl.ds(pl.multiple_of(me * z.chunk, 16), z.chunk), :] = low(total)
        for copy in small_copies():
            copy.start()
        for half in halves:
            state_sum(0, half)

    def edge_grad(half, m8):
        m = half * HALF + m8
        at = pl.multiple_of(m * z.edges, z.edges)
        _, _, pair_hot = pair_hots(idx[m], z.wpad)
        slot = slice(m8 * z.vpad, (m8 + 1) * z.vpad)
        grads = [e2[half, slot, w * units : (w + 1) * units] for w in range(z.wpad)]
        d_hidden = dot_tn(jnp.concatenate(grads, axis=0), pair_hot)
        d_pre = low(jnp.where(hid[m].astype(f32) > 0.0, d_hidden, 0.0))
        feats_m = r.feats_v[:, pl.ds(at, z.edges)]
        feats_m = jnp.concatenate([feats_m, jnp.ones((16, z.edges), bf16)], axis=0)
        return dot_nt(feats_m, d_pre)

    def half_grad(half, total):
        total = total + summed([edge_grad(half, m8) for m8 in range(HALF)])
        pl.when(half == 0)(between)
        return total

    total = lax.fori_loop(0, z.halves, half_grad, jnp.zeros((z.feats + 16, units), f32))
    w1_part, w1_in, w1_mid, w1_in2 = r.w1_part, r.w1_in, r.w1_mid, r.w1_in2
    w1_part[...] = total[: z.feats + 8]
    for at, peer in enumerate(row_peers):
        push(w1_part, w1_in.at[row], r.wr_send.at[at], r.wr_recv.at[row], ROW, peer)
    w1_in[row] = w1_part[...]

    if z.fused:
        total = r.dw_mid[0].astype(f32)
        for at in range(1, n_mol // 2):
            arrived(r.dw_in2.at[at], r.dw2_send.at[at], r.dw2_recv.at[at], MOL, partner)
            total = total + r.dw_in2[at].astype(f32)
        for i in range(rows):
            r.out_rows_v[:, i * LANES : (i + 1) * LANES] = total[i]
        store(r.out_rows_v, o.out_rows)
    else:
        store(dwp, o.out_rows)

    for peer in row_peers:
        arrived(w1_in.at[peer], r.wr_send.at[0], r.wr_recv.at[peer], ROW, peer)
    total = w1_in[0]
    for at in range(1, n_row):
        total = total + w1_in[at]
    w1_mid[...] = total
    for at, peer in enumerate(mol_peers):
        push(w1_mid, w1_in2.at[me], r.wm_send.at[at], r.wm_recv.at[me], MOL, peer)
    w1_in2[me] = w1_mid[...]

    for half in halves:
        collect(sred, r.ag_send, r.ag_recv, 0, half)
    r.state_grad_v[...] = rows_out(lambda half: gt[half] + sred[0, half].astype(f32))
    store(r.state_grad_v, o.state_grad)
    for peer in mol_peers:
        arrived(chunk_of(sm_red, peer), r.sa_send.at[0], r.sa_recv.at[peer], MOL, peer)
    store(sm_red, o.small_out)
    for peer in mol_peers:
        arrived(w1_in2.at[peer], r.wm_send.at[0], r.wm_recv.at[peer], MOL, peer)
    total = w1_in2[0]
    for at in range(1, n_mol):
        total = total + w1_in2[at]
    settle()
    w1_part[...] = total
    store(w1_part, o.w1_out)
    for at, (source, target) in enumerate(stored):
        pltpu.make_async_copy(source, target, r.osem.at[at]).wait()


def run_step(z, args, w2_all):
    (node_states, edge_feats, edge_src, edge_dst, atom_counts, edge_counts, mol_group, col_mask,
     cotangent, edge_in_state, edge_in_bias_state, edge_out_state, edge_out_bias_state,
     gate_in_state, gate_hidden_state, gate_bias_state) = args
    any_spec = pl.BlockSpec(memory_space=pl.ANY)
    v = pltpu.VMEM
    dma = pltpu.SemaphoreType.DMA
    rows, width, units, per = z.rows, z.width, z.units, z.per
    n_mol, n_row, halves = z.n_mol, z.n_row, z.halves
    half_rows, half_lanes = z.half_rows, z.half_lanes
    both = (LAYERS, halves)
    full = rows * HALF
    lines = (z.mols * z.edges // LANES, LANES)
    step_in = (rows, per, LANES)
    lane = np.arange(z.lanes)
    lane_mol, lane_v = lane // z.vpad, lane % z.vpad
    node = np.where(lane_v < z.cap, lane_mol * z.cap + lane_v, -1)
    perm_in = (np.arange(z.nodes)[:, None] == node[None, :]).astype(np.float32)
    row_at = np.arange(half_rows)
    row_lane = (row_at % HALF) * z.vpad + row_at // HALF
    perm = (row_lane[:, None] == np.arange(half_lanes)[None, :]).astype(np.float32)
    operands = Operands(
        nodes=(node_states, any_spec),
        feats_t=(edge_feats.T, any_spec),
        src=(edge_src.reshape(lines), any_spec),
        dst=(edge_dst.reshape(lines), any_spec),
        atoms=(atom_counts, any_spec),
        edges=(edge_counts, any_spec),
        group=(mol_group, any_spec),
        col_mask=(col_mask, any_spec),
        cot=(cotangent, any_spec),
        w1=(edge_in_state, any_spec),
        b1=(edge_in_bias_state, any_spec),
        w2=(edge_out_state if z.fused else w2_all, any_spec),
        b2=(edge_out_bias_state, any_spec),
        wi=(gate_in_state, any_spec),
        wh=(gate_hidden_state, any_spec),
        bg=(gate_bias_state, any_spec),
        perm_in_c=(jnp.asarray(perm_in, bf16), any_spec),
        perm_c=(jnp.asarray(perm, bf16), any_spec),
    )
    outs = [
        jax.ShapeDtypeStruct((z.nodes, width), f32),
        jax.ShapeDtypeStruct((z.nodes, width), f32),
        jax.ShapeDtypeStruct((per, rows * width), f32)
        if z.fused
        else jax.ShapeDtypeStruct((rows, units, width), bf16),
        jax.ShapeDtypeStruct((n_mol * z.chunk, width), bf16),
        jax.ShapeDtypeStruct((z.feats + 8, units), f32),
    ]
    row_sems = dma(both + (n_row,))
    mol_sems = dma((n_mol,))
    scratch = Scratch(
        nodes_v=v((z.nodes, width), bf16),
        feats_v=v((z.feats, z.mols * z.edges), bf16),
        src_v=v(lines, jnp.int32),
        dst_v=v(lines, jnp.int32),
        cot_v=v((z.nodes, width), bf16),
        w2_v=v((per, rows * width), f32),
        wi_v=v((width, 3 * width), f32),
        wh_v=v((width, 3 * width), f32),
        perm_in=v((z.nodes, z.lanes), bf16),
        perm=v((half_rows, half_lanes), bf16),
        w2s=v((rows, units, width), bf16),
        w2t=v((width, rows * units), bf16),
        stage=v(step_in, bf16),
        hid=v((z.mols, units, z.edges), bf16),
        idx=v((z.mols, 8, z.edges), f32),
        s2=v((halves, half_lanes, z.span), bf16),
        counts=v((halves, z.wpad, HALF, half_lanes), f32),
        cnt=v((halves, half_rows, half_lanes), bf16),
        t2=v(both + (full, z.span), bf16),
        d2=v((half_rows, rows * units), bf16),
        e2=v((halves, half_lanes, z.span), bf16),
        e_acc=v((halves, half_lanes, z.span), f32),
        dw_acc=v((width, rows * units), f32),
        ob_acc=v((rows, width), f32),
        live=v((halves, 8, half_lanes), f32),
        h=v((LAYERS + 1, halves, width, half_lanes), f32),
        hb=v(both + (width, half_lanes), bf16),
        hbw=v(both + (half_rows, width), bf16),
        hbw_t=v(both + (width, half_rows), bf16),
        gates=v(both + (2, 3 * width, half_lanes), f32),
        mt=v(both + (width, half_lanes), bf16),
        dmt=v(both + (full, half_lanes), bf16),
        dmn=v(both + (half_lanes, full), bf16),
        dm=v(both + (rows, half_lanes), bf16),
        dgi=v(both + (3 * width, half_lanes), bf16),
        dgh=v(both + (3 * width, half_lanes), bf16),
        wib=v((width, 3 * width), bf16),
        whb=v((width, 3 * width), bf16),
        wit=v((3 * width, width), bf16),
        wht=v((3 * width, width), bf16),
        bcol=v((2, 3 * width, LANES), f32),
        gt=v((halves, width, half_lanes), f32),
        spart=v(both + (width, half_lanes), bf16),
        rs_in=v(both + (n_row, rows, half_lanes), bf16),
        sred=v(both + (width, half_lanes), bf16),
        dwp=v((rows, units, width), bf16),
        dw_in=v((n_mol // 2,) + step_in, bf16),
        dw_mid=v((n_mol // 2,) + step_in, bf16),
        dw_in2=v((n_mol // 2,) + step_in, bf16),
        sm_part=v((n_mol * z.chunk, width), bf16),
        sm_in=v((n_mol, z.chunk, width), bf16),
        sm_red=v((n_mol * z.chunk, width), bf16),
        w1_part=v((z.feats + 8, units), f32),
        w1_in=v((n_row, z.feats + 8, units), f32),
        w1_mid=v((z.feats + 8, units), f32),
        w1_in2=v((n_mol, z.feats + 8, units), f32),
        col_mask_v=v(col_mask.shape, jnp.int32),
        w1_v=v(edge_in_state.shape[1:], f32),
        b1_v=v(edge_in_bias_state.shape, f32),
        bg_v=v(gate_bias_state.shape[1:], f32),
        b2_v=v(edge_out_bias_state.shape, f32),
        group_s=pltpu.SMEM(mol_group.shape, jnp.int32),
        edges_s=pltpu.SMEM(edge_counts.shape, jnp.int32),
        atoms_s=pltpu.SMEM(atom_counts.shape, jnp.int32),
        states_v=v((z.nodes, width), f32),
        state_grad_v=v((z.nodes, width), f32),
        out_rows_v=v((per, rows * width), f32),
        lsem=dma((len(operands),)),
        osem=dma((len(outs),)),
        w2_send=dma((PARTS, n_mol)),
        w2_recv=dma((PARTS, n_mol)),
        w2_fsend=dma((PARTS, n_mol)),
        m_send=row_sems,
        m_recv=row_sems,
        rs_send=row_sems,
        rs_recv=row_sems,
        ag_send=row_sems,
        ag_recv=row_sems,
        dw_send=mol_sems,
        dw_recv=mol_sems,
        dw2_send=mol_sems,
        dw2_recv=mol_sems,
        sm_send=mol_sems,
        sm_recv=mol_sems,
        sa_send=mol_sems,
        sa_recv=mol_sems,
        wr_send=dma((n_row,)),
        wr_recv=dma((n_row,)),
        wm_send=mol_sems,
        wm_recv=mol_sems,
    )
    return pl.pallas_call(
        functools.partial(step_kernel, z),
        out_shape=outs,
        in_specs=[spec for _, spec in operands],
        out_specs=[any_spec] * len(outs),
        scratch_shapes=list(scratch),
        compiler_params=pltpu.CompilerParams(
            collective_id=0, has_side_effects=True, vmem_limit_bytes=VMEM_BYTES
        ),
        name="step",
    )(*[array for array, _ in operands])


def nesterov(state, grad, rate, out):
    scaled = rate * grad
    moment = momentum_coef * state[1] + scaled
    weight = state[0] - (scaled + momentum_coef * moment)
    out[0] = weight
    out[1] = moment
    out[2] = average_decay * state[2] + (1.0 - average_decay) * weight


def nesterov_line(state, grad, rate, out):
    scaled = rate * grad
    moment = momentum_coef * state[1:2, :] + scaled
    weight = state[0:1, :] - (scaled + momentum_coef * moment)
    out[0:1, :] = weight
    out[1:2, :] = moment
    out[2:3, :] = average_decay * state[2:3, :] + (1.0 - average_decay) * weight


class Update(NamedTuple):
    states: Any
    state_grad: Any
    out_rows: Any
    small: Any
    w1_sum: Any
    w1: Any
    b1: Any
    w2: Any
    b2: Any
    wi: Any
    wh: Any
    bg: Any


class Updated(NamedTuple):
    states: Any
    state_grad: Any
    w1_g: Any
    w1_n: Any
    b1_g: Any
    b1_n: Any
    w2_g: Any
    w2_n: Any
    b2_g: Any
    b2_n: Any
    wi_g: Any
    wi_n: Any
    wh_g: Any
    wh_n: Any
    bg_g: Any
    bg_n: Any


def update_kernel(z, rates, *refs):
    n_in, n_out = len(Update._fields), len(Updated._fields)
    given, out = Update(*refs[:n_in]), Updated(*refs[n_in : n_in + n_out])
    refs = refs[n_in + n_out :]
    here, new = Update(*refs[:n_in]), Updated(*refs[n_in : n_in + n_out])
    in_sem, out_sem = refs[n_in + n_out :]
    rate_in, rate_out, rate_gate = rates
    width = z.width
    sent = []

    def send(source, target):
        copy = pltpu.make_async_copy(source, target, out_sem.at[len(sent)])
        copy.start()
        sent.append(copy)

    fetched = Update(
        *[pltpu.make_async_copy(given[at], here[at], in_sem.at[at]) for at in range(n_in)]
    )
    order = (fetched.wi, fetched.small, fetched.wh, fetched.w2, fetched.out_rows)
    passed = (fetched.states, fetched.state_grad)
    rest = (fetched.bg, fetched.b2, fetched.w1, fetched.b1, fetched.w1_sum)
    for copy in order + passed + rest:
        copy.start()

    def thirds(at):
        parts = [here.small[(3 * at + t) * width : (3 * at + t + 1) * width, :] for t in range(3)]
        return jnp.concatenate(parts, axis=1).astype(f32)

    fetched.wi.wait()
    fetched.small.wait()
    total = thirds(0)
    new.wi_g[...] = total
    nesterov(here.wi, total, rate_gate, new.wi_n)
    send(new.wi_g, out.wi_g)
    send(new.wi_n, out.wi_n)
    fetched.wh.wait()
    total = thirds(1)
    new.wh_g[...] = total
    nesterov(here.wh, total, rate_gate, new.wh_n)
    send(new.wh_g, out.wh_g)
    send(new.wh_n, out.wh_n)
    fetched.w2.wait()
    fetched.out_rows.wait()
    send(here.out_rows, out.w2_g)
    nesterov(here.w2, here.out_rows[...], rate_out, new.w2_n)
    send(new.w2_n, out.w2_n)
    for copy in passed + rest:
        copy.wait()
    send(here.states, out.states)
    send(here.state_grad, out.state_grad)
    lines = here.small[z.gate_rows : z.gate_rows + 16, :].astype(f32)
    total = jnp.concatenate(
        [
            jnp.concatenate([lines[3 * side + t : 3 * side + t + 1, :] for t in range(3)], axis=1)
            for side in range(2)
        ],
        axis=0,
    )
    new.bg_g[...] = total
    nesterov(here.bg, total, rate_gate, new.bg_n)
    send(new.bg_g, out.bg_g)
    send(new.bg_n, out.bg_n)
    total = here.small[z.gate_rows + 16 : z.gate_rows + 16 + z.rows, :].astype(f32)
    new.b2_g[...] = total
    total = jnp.concatenate([total[i : i + 1, :] for i in range(z.rows)], axis=1)
    nesterov_line(here.b2, total, rate_out, new.b2_n)
    send(new.b2_g, out.b2_g)
    send(new.b2_n, out.b2_n)
    total = here.w1_sum[: z.feats, :]
    new.w1_g[...] = total
    nesterov(here.w1, total, rate_in, new.w1_n)
    send(new.w1_g, out.w1_g)
    send(new.w1_n, out.w1_n)
    total = here.w1_sum[z.feats : z.feats + 1, :]
    new.b1_g[...] = total
    nesterov_line(here.b1, total, rate_in, new.b1_n)
    send(new.b1_g, out.b1_g)
    send(new.b1_n, out.b1_n)
    for copy in sent:
        copy.wait()


def per_device(mesh, *args):
    (node_states, edge_feats, edge_src, edge_dst, atom_counts, edge_counts, mol_group, col_mask,
     cotangent, edge_in_state, edge_in_bias_state, edge_out_state, edge_out_bias_state,
     gate_in_state, gate_hidden_state, gate_bias_state) = args
    z = Sizes(mesh, node_states, edge_feats, atom_counts, edge_in_state, edge_out_bias_state)
    w2_all = None
    if not z.fused:
        w2_all = lax.all_gather(low(edge_out_state[0]), "mol", axis=0, tiled=True)
        w2_all = w2_all.reshape(z.units, z.rows, z.width).swapaxes(0, 1)
    states, state_grad, out_rows, small, w1_sum = run_step(z, args, w2_all)
    if not z.fused:
        out_rows = out_rows.swapaxes(0, 1).reshape(z.units, z.rows * z.width)
        out_rows = lax.psum_scatter(out_rows, "mol", scatter_dimension=0, tiled=True).astype(f32)
    edges_all = edge_feats.shape[0] * z.n_mol
    nodes_all = z.nodes * z.n_mol
    rates = (
        z.feats ** (-0.5) / (0.2 * edges_all**0.5),
        (z.units * z.width * 8) ** (-0.5) / (0.4 * edges_all**0.5),
        z.width ** (-0.5) / (0.5 * nodes_all**0.5),
    )
    any_spec = pl.BlockSpec(memory_space=pl.ANY)
    operands = [
        states, state_grad, out_rows, small, w1_sum, edge_in_state, edge_in_bias_state,
        edge_out_state, edge_out_bias_state, gate_in_state, gate_hidden_state, gate_bias_state,
    ]
    outs = [
        states.shape, state_grad.shape, (z.feats, z.units), edge_in_state.shape,
        (1, z.units), edge_in_bias_state.shape, out_rows.shape, edge_out_state.shape,
        (z.rows, z.width), edge_out_bias_state.shape, (z.width, 3 * z.width), gate_in_state.shape,
        (z.width, 3 * z.width), gate_hidden_state.shape, (2, 3 * z.width), gate_bias_state.shape,
    ]
    results = pl.pallas_call(
        functools.partial(update_kernel, z, rates),
        out_shape=[jax.ShapeDtypeStruct(shape, f32) for shape in outs],
        in_specs=[any_spec] * len(operands),
        out_specs=[any_spec] * len(outs),
        scratch_shapes=[pltpu.VMEM(array.shape, array.dtype) for array in operands]
        + [pltpu.VMEM(shape, f32) for shape in outs]
        + [pltpu.SemaphoreType.DMA((len(operands),)), pltpu.SemaphoreType.DMA((len(outs),))],
        compiler_params=pltpu.CompilerParams(vmem_limit_bytes=VMEM_BYTES),
        name="update",
    )(*operands)
    results = list(results)
    results[4] = results[4].reshape(-1)
    results[8] = results[8].reshape(-1)
    return tuple(results)


def solution(mesh):
    return jax.shard_map(
        functools.partial(per_device, mesh),
        mesh=mesh,
        in_specs=(
            P(MOL, None),
            P(MOL, None),
            P(MOL),
            P(MOL),
            P(MOL),
            P(MOL),
            P(MOL),
            P(),
            P(MOL, None),
            P(),
            P(),
            P(None, MOL, ROW),
            P(None, ROW),
            P(),
            P(),
            P(),
        ),
        out_specs=(
            P(MOL, None),
            P(MOL, None),
            P(),
            P(),
            P(),
            P(),
            P(MOL, ROW),
            P(None, MOL, ROW),
            P(ROW),
            P(None, ROW),
            P(),
            P(),
            P(),
            P(),
            P(),
            P(),
        ),
        check_vma=False,
    )
```

profile of v0, /device:TPU:0, one launch (start us, length us, event | category | flops | bytes accessed | tf_op | source)
XLA Modules:
  0.0 66.4 jit_solution(12375706642742275048)
XLA Ops:
  0.7 62.7 %step.1 = (f32[464,128]{1,0:T(8,128)}, f32[464,128]{1,0:T(8,128)}, f32[16,4096]{1,0:T(8,128)}, bf16[896,128]{1,0:T(8,128)(2,1)}, f32[24,128]{1,0:T(8,128)}) custom-call(bf16[464,128]{1,0:T(8,128)(2,1)} %refs_0_.1, bf16[16,8192]{1,0:T(8,128)(2,1)} %bitcast.5, s32[64,128]{1,0:T(8,128)} %bitcast.6, s32[64,128]{1,0:T(8,128)} %bitcast.7, s32[16]{0:T(128)} %refs_4_.1, ...), custom_call_target="tpu_custom_call" | custom-call | tf_op jit(solution)/shard_map/step/pallas_call | solution.py:966
  63.4 3.1 %update.1 = (f32[464,128]{1,0:T(8,128)}, f32[464,128]{1,0:T(8,128)}, f32[16,128]{1,0:T(8,128)}, f32[3,16,128]{2,1,0:T(8,128)}, f32[1,128]{1,0:T(1,128)}, /*index...) custom-call(f32[464,128]{1,0:T(8,128)} %get-tuple-element.37.refs_0_, ...), custom_call_target="tpu_custom_call" | custom-call | tf_op jit(solution)/shard_map/update/pallas_call | solution.py:1144
where the time goes:
time: 66.6 us; the launch traced here: 66.4 us
  Pallas kernels  65.8 us (99%)
    pallas_call x1, Pallas kernels, run_step(): pl.pallas_call(functools.partial(step_kernel, z), out_shape=outs, in_spec...  62.7 us
    pallas_call x1, Pallas kernels, per_device(): pl.pallas_call(functools.partial(update_kernel, z, rates), out_shape=[jax...  3.09 us

commit v1 on v0

--- a/solution.py
+++ b/solution.py
@@ -12,7 +12,7 @@
 LAYERS = 2
 HALF = 8
 LANES = 128
-PARTS = 2
+PARTS = 1
 MOL, ROW = "mol", "row"
 MESH = pl.DeviceIdType.MESH
 VMEM_BYTES = 58 * 1024 * 1024
@@ -112,7 +112,6 @@
     perm_in: Any
     perm: Any
     w2s: Any
-    w2t: Any
     stage: Any
     hid: Any
     idx: Any
@@ -125,6 +124,8 @@
     e_acc: Any
     dw_acc: Any
     ob_acc: Any
+    gate_acc: Any
+    gate_bias_acc: Any
     live: Any
     h: Any
     hb: Any
@@ -156,7 +157,6 @@
     w1_part: Any
     w1_in: Any
     w1_mid: Any
-    w1_in2: Any
     col_mask_v: Any
     w1_v: Any
     b1_v: Any
@@ -297,7 +297,6 @@
     lane_mol = iota((1, z.lanes), 1) // z.vpad
     lane_v = lax.rem(iota((1, z.lanes), 1), z.vpad)
     half_mol = iota((HALF, z.half_lanes), 1) // z.vpad == iota((HALF, z.half_lanes), 0)
-    fold = hot(iota((rows, rows * HALF), 1) // HALF == iota((rows, rows * HALF), 0))
     tile_v = hot(lax.rem(iota((z.vpad, z.half_lanes), 1), z.vpad) == iota((z.vpad, z.half_lanes), 0))
     live_to = jnp.zeros((1, z.lanes), jnp.int32)
     for m in range(z.mols):
@@ -387,15 +386,13 @@
     def half_sums(half, carry):
         s2[half, :, z.cap * units :] = jnp.zeros((z.half_lanes, (z.wpad - z.cap) * units), bf16)
         for m8 in range(HALF):
-            if z.fused and m8 == HALF - 2:
-                pl.when(half == z.halves - 1)(functools.partial(forward_part, 0))
             one_molecule(half, m8)
         r.cnt[half] = low(counts[half].reshape(z.half_rows, z.half_lanes))
         return carry
 
     lax.fori_loop(0, z.halves, half_sums, 0)
     if z.fused:
-        for part in range(1, PARTS):
+        for part in range(PARTS):
             forward_part(part)
 
     h, hb, hbw, hbw_t = r.h, r.hb, r.hbw, r.hbw_t
@@ -424,7 +421,7 @@
     if not z.fused:
         in_w2.wait()
 
-    t2, mt, gates, w2t = r.t2, r.mt, r.gates, r.w2t
+    t2, mt, gates = r.t2, r.mt, r.gates
 
     def two(at):
         return slice(at * 2 * units, (at + 1) * 2 * units)
@@ -453,8 +450,7 @@
         bias = dot(low(dot_nt(b2_low, state)), r.cnt[half])
         full = dot_nt(t2[layer, half], s2[half]).reshape(rows, HALF, z.half_lanes)
         full = jnp.where(half_mol[None], full + bias[:, None, :], 0.0)
-        full = low(full.reshape(rows * HALF, z.half_lanes))
-        mt[layer, half, pl.ds(row_at, rows), :] = low(dot(fold, full))
+        mt[layer, half, pl.ds(row_at, rows), :] = low(jnp.sum(full, axis=1))
         share(mt, r.m_send, r.m_recv, layer, half)
 
     def row_pushes(ref, send, recv, layer, half):
@@ -531,8 +527,8 @@
     def state_part(layer, half):
         biases = bias_rows(layer, half)
         r.ob_acc[...] += dot(biases, hbw[layer, half])
-        back = dot_nt(w2t[...], d2[...]) + dot_tn(b2_low, biases)
-        spart[layer, half] = low(dot(low(back), r.perm[...]))
+        back = dot(d2[...], w2s[...].reshape(rows * units, width)) + dot_tn(biases, b2_low)
+        spart[layer, half] = low(dot_tn(low(back), r.perm[...]))
         for copy in part_pushes(layer, half):
             copy.start()
 
@@ -575,7 +571,7 @@
         for copy in small_copies():
             copy.wait_send()
         if z.fused:
-            for copy in owner_copies():
+            for copy in pair_copies():
                 copy.wait_send()
             for part in range(PARTS):
                 for copy in forwards(part):
@@ -620,8 +616,6 @@
         for side in range(2):
             bcol[side] = jnp.broadcast_to(bias_t[:, side : side + 1], (3 * width, LANES))
         rows_in(r.cot_v[...], r.gt)
-        for i in range(rows):
-            w2t[:, i * units : (i + 1) * units] = w2s[i].T
         for half in halves:
             state_side(0, half)
 
@@ -648,6 +642,18 @@
 
     last = LAYERS - 1
 
+    ones = jnp.ones((8, z.lanes), bf16)
+
+    def beside(ref, layer):
+        return jnp.concatenate([ref[layer, half] for half in halves], axis=1)
+
+    def gate_sums(layer):
+        sums = []
+        for at, (side, grads) in enumerate(((mt, dgi), (hb, dgh))):
+            grads = beside(grads, layer)
+            sums.append((dot_nt(beside(side, layer), grads), dot_nt(ones, grads)))
+        return sums
+
     def back_half(layer, half):
         @pl.when(layer == last)
         def _():
@@ -665,52 +671,49 @@
 
     def pair_half(layer, half):
         pair_grad(layer, half)
-
-        @pl.when(layer == last)
-        def _():
-            state_sum(last, half)
+        pl.when(layer == last)(functools.partial(state_sum, last, half))
+
+    theirs = [lax.rem(partner + 2 * step, n_mol) for step in range(n_mol // 2)]
+    ours = [lax.rem(me + 2 * step, n_mol) for step in range(n_mol // 2)]
+
+    def pair_copies():
+        return [
+            remote(block_of(dwp, owner), r.dw_in.at[at], r.dw_send.at[at], r.dw_recv.at[at], MOL, partner)
+            for at, owner in enumerate(theirs)
+        ]
+
+    def weight_out():
+        for i in range(rows):
+            dwp[i] = low(dw_acc[:, i * units : (i + 1) * units]).T
+        if z.fused:
+            for copy in pair_copies():
+                copy.start()
 
     def backward_layer(t, carry):
         layer = last - t
         lax.fori_loop(0, z.halves, lambda half, c: back_half(layer, half) or c, 0)
+        pl.when(layer == 0)(weight_out)
         lax.fori_loop(0, z.halves, lambda half, c: pair_half(layer, half) or c, 0)
 
         @pl.when(layer == last)
         def _():
             r.states_v[...] = rows_out(lambda half: h[LAYERS, half])
             store(r.states_v, o.states)
+            for at, (weight, bias) in enumerate(gate_sums(last)):
+                r.gate_acc[at], r.gate_bias_acc[at] = weight, bias
 
         return carry
 
     lax.fori_loop(0, LAYERS, backward_layer, 0)
 
-    for i in range(rows):
-        dwp[i] = low(dw_acc[:, i * units : (i + 1) * units].T)
-    theirs = [lax.rem(partner + 2 * step, n_mol) for step in range(n_mol // 2)]
-    ours = [lax.rem(me + 2 * step, n_mol) for step in range(n_mol // 2)]
-    if z.fused:
-        for at, owner in enumerate(theirs):
-            push(block_of(dwp, owner), r.dw_in.at[at], r.dw_send.at[at], r.dw_recv.at[at], MOL, partner)
-
-    sm_part, sm_in, sm_red = r.sm_part, r.sm_in, r.sm_red
-    every = [(layer, half) for layer in range(LAYERS) for half in halves]
-
-    def summed(pieces):
-        return functools.reduce(jnp.add, pieces)
-
-    def beside(ref):
-        return jnp.concatenate([ref[e] for e in every], axis=1)
-
-    for at, (side, grads) in enumerate(((mt, dgi), (hb, dgh))):
-        total = dot_nt(beside(side), beside(grads))
+    sm_part, sm_in = r.sm_part, r.sm_in
+    bias_lines = []
+    for at, (weight, bias) in enumerate(gate_sums(0)):
+        weight, bias = weight + r.gate_acc[at], bias + r.gate_bias_acc[at]
         for third in range(3):
             first = (3 * at + third) * width
-            sm_part[first : first + width, :] = low(total[:, third * width : (third + 1) * width])
-    ones = jnp.ones((8, len(every) * z.half_lanes), bf16)
-    bias_lines = []
-    for grads in (dgi, dgh):
-        total = dot_nt(ones, beside(grads))
-        bias_lines += [total[0:1, third * width : (third + 1) * width] for third in range(3)]
+            sm_part[first : first + width, :] = low(weight[:, third * width : (third + 1) * width])
+        bias_lines += [bias[0:1, third * width : (third + 1) * width] for third in range(3)]
     bias_lines.append(jnp.zeros((10, width), f32))
     sm_part[z.gate_rows : z.gate_rows + 16, :] = low(jnp.concatenate(bias_lines, axis=0))
     sm_part[z.gate_rows + 16 : z.small_rows, :] = low(r.ob_acc[...])
@@ -722,38 +725,26 @@
 
     for at, peer in enumerate(mol_peers):
         push(chunk_of(sm_part, peer), sm_in.at[me], r.sm_send.at[at], r.sm_recv.at[me], MOL, peer)
-
-    def owner_copies():
+    if z.fused:
+        for at, owner in enumerate(ours):
+            arrived(r.dw_in.at[at], r.dw_send.at[at], r.dw_recv.at[at], MOL, partner)
+            own = dwp[:, pl.ds(pl.multiple_of(owner * per, 16), per), :].astype(f32)
+            r.dw_mid[at] = low(own + r.dw_in[at].astype(f32))
+            if at > 0:
+                push(r.dw_mid.at[at], r.dw_in2.at[at], r.dw2_send.at[at], r.dw2_recv.at[at], MOL, owner)
+
+    def small_copies():
         return [
-            remote(r.dw_mid.at[at], r.dw_in2.at[at], r.dw2_send.at[at], r.dw2_recv.at[at], MOL, owner)
-            for at, owner in enumerate(ours)
-            if at > 0
-        ]
-
-    def small_copies():
-        mine = chunk_of(sm_red, me)
-        return [
-            remote(mine, mine, r.sa_send.at[at], r.sa_recv.at[me], MOL, peer)
+            remote(r.sm_red, chunk_of(o.small_out, me), r.sa_send.at[at], r.sa_recv.at[me], MOL, peer)
             for at, peer in enumerate(mol_peers)
         ]
 
     def between():
-        if z.fused:
-            for at, owner in enumerate(ours):
-                arrived(r.dw_in.at[at], r.dw_send.at[at], r.dw_recv.at[at], MOL, partner)
-                own = dwp[:, pl.ds(pl.multiple_of(owner * per, 16), per), :].astype(f32)
-                r.dw_mid[at] = low(own + r.dw_in[at].astype(f32))
-                if at > 0:
-                    owner_copies()[at - 1].start()
-        total = sm_part[pl.ds(pl.multiple_of(me * z.chunk, 16), z.chunk), :].astype(f32)
-        for peer in mol_peers:
-            arrived(sm_in.at[peer], r.sm_send.at[0], r.sm_recv.at[peer], MOL, peer)
-            total = total + sm_in[peer].astype(f32)
-        sm_red[pl.ds(pl.multiple_of(me * z.chunk, 16), z.chunk), :] = low(total)
-        for copy in small_copies():
-            copy.start()
         for half in halves:
             state_sum(0, half)
+
+    def summed(pieces):
+        return functools.reduce(jnp.add, pieces)
 
     def edge_grad(half, m8):
         m = half * HALF + m8
@@ -765,20 +756,44 @@
         d_pre = low(jnp.where(hid[m].astype(f32) > 0.0, d_hidden, 0.0))
         feats_m = r.feats_v[:, pl.ds(at, z.edges)]
         feats_m = jnp.concatenate([feats_m, jnp.ones((16, z.edges), bf16)], axis=0)
-        return dot_nt(feats_m, d_pre)
+        return dot_nt(d_pre, feats_m)
 
     def half_grad(half, total):
         total = total + summed([edge_grad(half, m8) for m8 in range(HALF)])
         pl.when(half == 0)(between)
         return total
 
-    total = lax.fori_loop(0, z.halves, half_grad, jnp.zeros((z.feats + 16, units), f32))
-    w1_part, w1_in, w1_mid, w1_in2 = r.w1_part, r.w1_in, r.w1_mid, r.w1_in2
+    total = lax.fori_loop(0, z.halves, half_grad, jnp.zeros((units, z.feats + 16), f32))
+    w1_part, w1_in, w1_mid = r.w1_part, r.w1_in, r.w1_mid
+    total = jnp.concatenate([total, jnp.zeros((units, LANES - z.feats - 16), f32)], axis=1).T
     w1_part[...] = total[: z.feats + 8]
     for at, peer in enumerate(row_peers):
         push(w1_part, w1_in.at[row], r.wr_send.at[at], r.wr_recv.at[row], ROW, peer)
     w1_in[row] = w1_part[...]
 
+    total = sm_part[pl.ds(pl.multiple_of(me * z.chunk, 16), z.chunk), :].astype(f32)
+    for peer in mol_peers:
+        arrived(sm_in.at[peer], r.sm_send.at[0], r.sm_recv.at[peer], MOL, peer)
+        total = total + sm_in[peer].astype(f32)
+    r.sm_red[...] = low(total)
+    for copy in small_copies():
+        copy.start()
+    store(r.sm_red, chunk_of(o.small_out, me))
+    for peer in row_peers:
+        arrived(w1_in.at[peer], r.wr_send.at[0], r.wr_recv.at[peer], ROW, peer)
+    total = w1_in[0]
+    for at in range(1, n_row):
+        total = total + w1_in[at]
+    w1_mid[...] = total
+    for at, peer in enumerate(mol_peers):
+        push(w1_mid, o.w1_out.at[me], r.wm_send.at[at], r.wm_recv.at[me], MOL, peer)
+    store(w1_mid, o.w1_out.at[me])
+
+    for half in halves:
+        collect(sred, r.ag_send, r.ag_recv, 0, half)
+    r.state_grad_v[...] = rows_out(lambda half: gt[half] + sred[0, half].astype(f32))
+    store(r.state_grad_v, o.state_grad)
+    settle()
     if z.fused:
         total = r.dw_mid[0].astype(f32)
         for at in range(1, n_mol // 2):
@@ -789,32 +804,10 @@
         store(r.out_rows_v, o.out_rows)
     else:
         store(dwp, o.out_rows)
-
-    for peer in row_peers:
-        arrived(w1_in.at[peer], r.wr_send.at[0], r.wr_recv.at[peer], ROW, peer)
-    total = w1_in[0]
-    for at in range(1, n_row):
-        total = total + w1_in[at]
-    w1_mid[...] = total
-    for at, peer in enumerate(mol_peers):
-        push(w1_mid, w1_in2.at[me], r.wm_send.at[at], r.wm_recv.at[me], MOL, peer)
-    w1_in2[me] = w1_mid[...]
-
-    for half in halves:
-        collect(sred, r.ag_send, r.ag_recv, 0, half)
-    r.state_grad_v[...] = rows_out(lambda half: gt[half] + sred[0, half].astype(f32))
-    store(r.state_grad_v, o.state_grad)
     for peer in mol_peers:
-        arrived(chunk_of(sm_red, peer), r.sa_send.at[0], r.sa_recv.at[peer], MOL, peer)
-    store(sm_red, o.small_out)
+        arrived(o.w1_out.at[peer], r.wm_send.at[0], r.wm_recv.at[peer], MOL, peer)
     for peer in mol_peers:
-        arrived(w1_in2.at[peer], r.wm_send.at[0], r.wm_recv.at[peer], MOL, peer)
-    total = w1_in2[0]
-    for at in range(1, n_mol):
-        total = total + w1_in2[at]
-    settle()
-    w1_part[...] = total
-    store(w1_part, o.w1_out)
+        arrived(chunk_of(o.small_out, peer), r.sa_send.at[0], r.sa_recv.at[peer], MOL, peer)
     for at, (source, target) in enumerate(stored):
         pltpu.make_async_copy(source, target, r.osem.at[at]).wait()
 
@@ -867,7 +860,7 @@
         if z.fused
         else jax.ShapeDtypeStruct((rows, units, width), bf16),
         jax.ShapeDtypeStruct((n_mol * z.chunk, width), bf16),
-        jax.ShapeDtypeStruct((z.feats + 8, units), f32),
+        jax.ShapeDtypeStruct((n_mol, z.feats + 8, units), f32),
     ]
     row_sems = dma(both + (n_row,))
     mol_sems = dma((n_mol,))
@@ -883,7 +876,6 @@
         perm_in=v((z.nodes, z.lanes), bf16),
         perm=v((half_rows, half_lanes), bf16),
         w2s=v((rows, units, width), bf16),
-        w2t=v((width, rows * units), bf16),
         stage=v(step_in, bf16),
         hid=v((z.mols, units, z.edges), bf16),
         idx=v((z.mols, 8, z.edges), f32),
@@ -896,6 +888,8 @@
         e_acc=v((halves, half_lanes, z.span), f32),
         dw_acc=v((width, rows * units), f32),
         ob_acc=v((rows, width), f32),
+        gate_acc=v((2, width, 3 * width), f32),
+        gate_bias_acc=v((2, 8, 3 * width), f32),
         live=v((halves, 8, half_lanes), f32),
         h=v((LAYERS + 1, halves, width, half_lanes), f32),
         hb=v(both + (width, half_lanes), bf16),
@@ -923,11 +917,10 @@
         dw_in2=v((n_mol // 2,) + step_in, bf16),
         sm_part=v((n_mol * z.chunk, width), bf16),
         sm_in=v((n_mol, z.chunk, width), bf16),
-        sm_red=v((n_mol * z.chunk, width), bf16),
+        sm_red=v((z.chunk, width), bf16),
         w1_part=v((z.feats + 8, units), f32),
         w1_in=v((n_row, z.feats + 8, units), f32),
         w1_mid=v((z.feats + 8, units), f32),
-        w1_in2=v((n_mol, z.feats + 8, units), f32),
         col_mask_v=v(col_mask.shape, jnp.int32),
         w1_v=v(edge_in_state.shape[1:], f32),
         b1_v=v(edge_in_bias_state.shape, f32),
@@ -940,7 +933,7 @@
         state_grad_v=v((z.nodes, width), f32),
         out_rows_v=v((per, rows * width), f32),
         lsem=dma((len(operands),)),
-        osem=dma((len(outs),)),
+        osem=dma((8,)),
         w2_send=dma((PARTS, n_mol)),
         w2_recv=dma((PARTS, n_mol)),
         w2_fsend=dma((PARTS, n_mol)),
@@ -1096,12 +1089,13 @@
     nesterov_line(here.b2, total, rate_out, new.b2_n)
     send(new.b2_g, out.b2_g)
     send(new.b2_n, out.b2_n)
-    total = here.w1_sum[: z.feats, :]
+    w1_sum = sum(here.w1_sum[at] for at in range(z.n_mol))
+    total = w1_sum[: z.feats, :]
     new.w1_g[...] = total
     nesterov(here.w1, total, rate_in, new.w1_n)
     send(new.w1_g, out.w1_g)
     send(new.w1_n, out.w1_n)
-    total = here.w1_sum[z.feats : z.feats + 1, :]
+    total = w1_sum[z.feats : z.feats + 1, :]
     new.b1_g[...] = total
     nesterov_line(here.b1, total, rate_in, new.b1_n)
     send(new.b1_g, out.b1_g)

time: 66.6 us -> 60.4 us (0.907)
  Pallas kernels: 65.8 us -> 59.6 us
    pallas_call x1, Pallas kernels: 62.7 us -> 56.5 us  [run_step(): pl.pallas_call(functools.partial(step_kernel, z), out_shape=outs, in_spec...]
where the time goes in v1:
time: 60.4 us; the launch traced here: 60.2 us
  Pallas kernels  59.6 us (99%)
  between operations  0.66 us (1%)
    pallas_call x1, Pallas kernels, run_step(): pl.pallas_call(functools.partial(step_kernel, z), out_shape=outs, in_spec...  56.5 us
    pallas_call x1, Pallas kernels, per_device(): pl.pallas_call(functools.partial(update_kernel, z, rates), out_shape=[jax...  3.09 us

profile of v1, /device:TPU:0, one launch (start us, length us, event | category | flops | bytes accessed | tf_op | source)
XLA Modules:
  0.0 60.2 jit_solution(1498561435314286513)
XLA Ops:
  0.7 56.5 %step.1 = (f32[464,128]{1,0:T(8,128)}, f32[464,128]{1,0:T(8,128)}, f32[16,4096]{1,0:T(8,128)}, bf16[896,128]{1,0:T(8,128)(2,1)}, f32[8,24,128]{2,1,0:T(8,128)}) custom-call(bf16[464,128]{1,0:T(8,128)(2,1)} %refs_0_.1, bf16[16,8192]{1,0:T(8,128)(2,1)} %bitcast.5, s32[64,128]{1,0:T(8,128)} %bitcast.6, s32[64,128]{1,0:T(8,128)} %bitcast.7, s32[16]{0:T(128)} %refs_4_.1, ...), custom_call_target="tpu_custom_call" | custom-call | tf_op jit(solution)/shard_map/step/pallas_call | solution.py:959
  57.1 3.1 %update.1 = (f32[464,128]{1,0:T(8,128)}, f32[464,128]{1,0:T(8,128)}, f32[16,128]{1,0:T(8,128)}, f32[3,16,128]{2,1,0:T(8,128)}, f32[1,128]{1,0:T(1,128)}, /*index...) custom-call(f32[464,128]{1,0:T(8,128)} %get-tuple-element.37.refs_0_, ...), custom_call_target="tpu_custom_call" | custom-call | tf_op jit(solution)/shard_map/update/pallas_call | solution.py:1138

commit v2 on v1

--- a/solution.py
+++ b/solution.py
@@ -207,7 +207,18 @@
     def others(index, count):
         return [lax.rem(index + step, count) for step in range(1, count)]
 
-    mol_peers, row_peers = others(me, n_mol), others(row, n_row)
+    def far_first(index, count):
+        upper, mirror = lax.div(2 * index, count), count - 1 - index
+        from_low = [at + lax.div(at + count - index, count) for at in range(count - 1)]
+        from_high = [count - 1 - at - lax.div(at + count - mirror, count) for at in range(count - 1)]
+        return [upper * low_at + (1 - upper) * high_at for low_at, high_at in zip(from_low, from_high)]
+
+    def flipped(index, mask):
+        bits = [1 << b for b in range(n_mol.bit_length() - 1)]
+        return sum(bit * lax.rem(lax.div(index, bit) + (1 if mask & bit else 0), 2) for bit in bits)
+
+    by_distance = sorted(range(1, n_mol), key=lambda mask: (-(mask // 2).bit_count(), -mask))
+    mol_peers, row_peers = [flipped(me, mask) for mask in by_distance], far_first(row, n_row)
 
     def remote(source, target, send, recv, axis, device):
         return pltpu.make_async_remote_copy(
@@ -263,8 +274,8 @@
 
     w2s, stage = r.w2s, r.stage
     partner = me + 1 - 2 * lax.rem(me, 2)
-    same = [lax.rem(me + 2 * step, n_mol) for step in range(1, n_mol // 2)]
-    same_of_partner = [lax.rem(partner + 2 * step, n_mol) for step in range(1, n_mol // 2)]
+    same = [flipped(me, mask) for mask in by_distance if mask % 2 == 0]
+    same_of_partner = [flipped(partner, mask) for mask in by_distance if mask % 2 == 0]
 
     some = rows // PARTS
 

time: 60.4 us -> 59.5 us (0.985)
  Pallas kernels: 59.6 us -> 58.7 us
    pallas_call x1, Pallas kernels: 56.5 us -> 55.6 us  [run_step(): pl.pallas_call(functools.partial(step_kernel, z), out_shape=outs, in_spec...]
where the time goes in v2:
time: 59.5 us; the launch traced here: 59.3 us
  Pallas kernels  58.7 us (99%)
  between operations  0.66 us (1%)
    pallas_call x1, Pallas kernels, run_step(): pl.pallas_call(functools.partial(step_kernel, z), out_shape=outs, in_spec...  55.6 us
    pallas_call x1, Pallas kernels, per_device(): pl.pallas_call(functools.partial(update_kernel, z, rates), out_shape=[jax...  3.09 us

profile of v2, /device:TPU:0, one launch (start us, length us, event | category | flops | bytes accessed | tf_op | source)
XLA Modules:
  0.0 59.3 jit_solution(3129180525774938542)
XLA Ops:
  0.7 55.6 %step.1 = (f32[464,128]{1,0:T(8,128)}, f32[464,128]{1,0:T(8,128)}, f32[16,4096]{1,0:T(8,128)}, bf16[896,128]{1,0:T(8,128)(2,1)}, f32[8,24,128]{2,1,0:T(8,128)}) custom-call(bf16[464,128]{1,0:T(8,128)(2,1)} %refs_0_.1, bf16[16,8192]{1,0:T(8,128)(2,1)} %bitcast.5, s32[64,128]{1,0:T(8,128)} %bitcast.6, s32[64,128]{1,0:T(8,128)} %bitcast.7, s32[16]{0:T(128)} %refs_4_.1, ...), custom_call_target="tpu_custom_call" | custom-call | tf_op jit(solution)/shard_map/step/pallas_call | solution.py:970
  56.2 3.1 %update.1 = (f32[464,128]{1,0:T(8,128)}, f32[464,128]{1,0:T(8,128)}, f32[16,128]{1,0:T(8,128)}, f32[3,16,128]{2,1,0:T(8,128)}, f32[1,128]{1,0:T(1,128)}, /*index...) custom-call(f32[464,128]{1,0:T(8,128)} %get-tuple-element.37.refs_0_, ...), custom_call_target="tpu_custom_call" | custom-call | tf_op jit(solution)/shard_map/update/pallas_call | solution.py:1149

commit v3 on v2

--- a/solution.py
+++ b/solution.py
@@ -316,9 +316,6 @@
     for half in halves:
         lanes = slice(half * z.half_lanes, (half + 1) * z.half_lanes)
         r.live[half] = jnp.broadcast_to(live_all[:, lanes], (8, z.half_lanes))
-    r.e_acc[...] = jnp.zeros(r.e_acc.shape, f32)
-    r.dw_acc[...] = jnp.zeros(r.dw_acc.shape, f32)
-    r.ob_acc[...] = jnp.zeros(r.ob_acc.shape, f32)
 
     mask_cols = jnp.concatenate(
         [r.col_mask_v[...].astype(f32), jnp.zeros((8 - a.col_mask.shape[0], z.feats), f32)], axis=0
@@ -615,6 +612,9 @@
             e2[half, :, at] = low(total)
 
     def gate_weights():
+        r.e_acc[...] = jnp.zeros(r.e_acc.shape, f32)
+        r.dw_acc[...] = jnp.zeros(r.dw_acc.shape, f32)
+        r.ob_acc[...] = jnp.zeros(r.ob_acc.shape, f32)
         in_wi.wait()
         in_wh.wait()
         wib[...] = low(r.wi_v[...])
@@ -684,8 +684,7 @@
         pair_grad(layer, half)
         pl.when(layer == last)(functools.partial(state_sum, last, half))
 
-    theirs = [lax.rem(partner + 2 * step, n_mol) for step in range(n_mol // 2)]
-    ours = [lax.rem(me + 2 * step, n_mol) for step in range(n_mol // 2)]
+    theirs, ours = [partner] + same_of_partner, [me] + same
 
     def pair_copies():
         return [

time: 59.5 us -> 59.8 us (level)
  no operation moved by 1% of the time
where the time goes in v3:
time: 59.8 us; the launch traced here: 59.7 us
  Pallas kernels  59 us (99%)
  between operations  0.66 us (1%)
    pallas_call x1, Pallas kernels, run_step(): pl.pallas_call(functools.partial(step_kernel, z), out_shape=outs, in_spec...  55.9 us
    pallas_call x1, Pallas kernels, per_device(): pl.pallas_call(functools.partial(update_kernel, z, rates), out_shape=[jax...  3.09 us

profile of v3, /device:TPU:0, one launch (start us, length us, event | category | flops | bytes accessed | tf_op | source)
XLA Modules:
  0.0 59.7 jit_solution(7502185908082300667)
XLA Ops:
  0.7 55.9 %step.1 = (f32[464,128]{1,0:T(8,128)}, f32[464,128]{1,0:T(8,128)}, f32[16,4096]{1,0:T(8,128)}, bf16[896,128]{1,0:T(8,128)(2,1)}, f32[8,24,128]{2,1,0:T(8,128)}) custom-call(bf16[464,128]{1,0:T(8,128)(2,1)} %refs_0_.1, bf16[16,8192]{1,0:T(8,128)(2,1)} %bitcast.5, s32[64,128]{1,0:T(8,128)} %bitcast.6, s32[64,128]{1,0:T(8,128)} %bitcast.7, s32[16]{0:T(128)} %refs_4_.1, ...), custom_call_target="tpu_custom_call" | custom-call | tf_op jit(solution)/shard_map/step/pallas_call | solution.py:969
  56.6 3.1 %update.1 = (f32[464,128]{1,0:T(8,128)}, f32[464,128]{1,0:T(8,128)}, f32[16,128]{1,0:T(8,128)}, f32[3,16,128]{2,1,0:T(8,128)}, f32[1,128]{1,0:T(1,128)}, /*index...) custom-call(f32[464,128]{1,0:T(8,128)} %get-tuple-element.37.refs_0_, ...), custom_call_target="tpu_custom_call" | custom-call | tf_op jit(solution)/shard_map/update/pallas_call | solution.py:1148
